TPU v7x, 128 devices: a whole 4x4x4 slice. The times are simulated.
128 devices in a mesh: dp: 64 (over z, y, x), inner: 2 (over core).
Axes of the slice: x: 4, y: 4, z: 4, core: 2. Of those that a mesh axis runs over, the one named last changes fastest.
Arguments:
- latent_pool: bfloat16 [8192, 64, 576], P('dp', 'inner'), may hold values from -7 to 7
- block_table: int32 [2, 512, 8], P(None, 'dp'), may hold values from 0 to 127, as said below
- cache_lengths: int32 [2, 512], P(None, 'dp'), may hold values from 2 to 512
- queries: bfloat16 [2, 512, 128, 576], P(None, 'dp', 'inner'), may hold values from -400 to 400
- hidden_states: bfloat16 [2, 512, 3584], P(None, 'dp', 'inner'), may hold values from -6 to 6
- expert_ids: int32 [2, 512, 8], P(None, 'dp'), may hold values from 0 to 63, all different within a row; in each aligned block of 8 rows (0 to 7, 8 to 15, ..., all dimensions but the last counted through in order) at most 2 rows name the same one
- gate_weights: float32 [2, 512, 8], P(None, 'dp'), may hold values from 0.05 to 0.6
- w_gate: bfloat16 [64, 3584, 1024], P('dp', None, 'inner'), may hold values from -0.09375 to 0.09375
- w_up: bfloat16 [64, 3584, 1024], P('dp', None, 'inner'), may hold values from -0.09375 to 0.09375
- w_down: bfloat16 [64, 1024, 3584], P('dp', 'inner'), may hold values from -0.1875 to 0.1875
Outputs:
- context: bfloat16 [2, 512, 128, 512], P(None, 'dp', 'inner')
- moe_out: bfloat16 [2, 512, 3584], P(None, 'dp', 'inner')
Inputs may be any that keep to these rules, and one draw needn't show every extreme that they name: `block_table`: over both micro-batches, the 128 entries of the sessions of one dp index name every slot exactly once; entries of blocks past a session's length are never read. `expert_ids`: in each micro-batch, at most 2 of the tokens of one dp index name the same expert, and no token names one expert twice.
All inputs are finite; a program needn't handle non-finite values.
Results may differ from a plain program's by a relative error of at most 0.018.
Values may be sent and summed in bfloat16 or wider, within the bound.
A program may use at most 128 MiB of HBM per device.

v0:
```python
import jax
import jax.numpy as jnp
from jax import lax
from jax.sharding import PartitionSpec as P

KV = 512


softmax_scale = 192 ** (-0.5)


def route_tables(expert_ids, gate_weights, experts, room):
    batches, row_count, picks = expert_ids.shape
    flattened = expert_ids.reshape(batches, row_count * picks)
    expert_names = jnp.arange(experts, dtype=jnp.int32)
    member = (flattened[:, :, None] == expert_names[None, None, :]).astype(jnp.int32)
    earlier = jnp.cumsum(member, axis=1) - member
    slot_of = jnp.sum(earlier * member, axis=2)
    target = flattened * room + slot_of
    columns = jnp.arange(experts * room, dtype=jnp.int32)
    matches = (target[:, :, None] == columns[None, None, :]).reshape(
        batches, row_count, picks, experts * room
    )
    placing = jnp.sum(matches.astype(jnp.float32), axis=2).astype(jnp.bfloat16)
    weighting = jnp.sum(jnp.where(matches, gate_weights[..., None], 0.0), axis=2)
    return (placing, weighting)


def moe_round(tokens, expert_ids, gate_weights, w_gate, w_up, w_down):
    batches, row_count, slice_width = tokens.shape
    experts = lax.axis_size("dp")
    room = max(2, 2 * row_count * expert_ids.shape[2] // experts)
    placing, weighting = route_tables(expert_ids, gate_weights, experts, room)
    gate_rows = w_gate[0]
    up_rows = w_up[0]
    down_rows = w_down[0]
    outgoing = jnp.einsum(
        "msq,msd->qmd", placing, tokens, preferred_element_type=jnp.float32
    ).astype(jnp.bfloat16)
    outgoing = outgoing.reshape(experts, room * batches, slice_width)
    arrived = lax.all_to_all(outgoing, "dp", split_axis=0, concat_axis=0, tiled=True)
    lined = arrived.reshape(experts * room * batches, slice_width)
    columns_in = lax.all_gather(lined, "inner", axis=1, tiled=True)
    gate_sum = jnp.dot(columns_in, gate_rows, preferred_element_type=jnp.float32)
    up_sum = jnp.dot(columns_in, up_rows, preferred_element_type=jnp.float32)
    hidden = (jax.nn.silu(gate_sum) * up_sum).astype(jnp.bfloat16)
    summed = lax.psum_scatter(
        lax.dot_general(
            down_rows, hidden, (((0,), (1,)), ((), ())), preferred_element_type=jnp.float32
        ).astype(jnp.bfloat16),
        "inner",
        scatter_dimension=0,
        tiled=True,
    ).astype(jnp.float32)
    outbound = summed.astype(jnp.bfloat16).reshape(summed.shape[0], experts, room * batches)
    returned = lax.all_to_all(outbound, "dp", split_axis=1, concat_axis=1, tiled=True)
    mixed = returned.reshape(returned.shape[0], experts, room, batches).astype(jnp.float32)
    combined = jnp.einsum(
        "decm,msec->msd",
        mixed,
        weighting.reshape(batches, row_count, experts, room),
        precision=lax.Precision.HIGHEST,
    )
    return combined.astype(jnp.bfloat16)


def on_device(
    latent_pool,
    block_table,
    cache_lengths,
    queries,
    hidden_states,
    expert_ids,
    gate_weights,
    w_gate,
    w_up,
    w_down,
):
    groups = lax.axis_size("inner")
    inner_rank = lax.axis_index("inner")
    resident = lax.all_to_all(latent_pool, "dp", split_axis=0, concat_axis=0, tiled=True)
    block_dev = resident.shape[1]
    latent_width = resident.shape[2]
    batches, sessions_dev, blocks = block_table.shape
    cached = resident[block_table].reshape(batches, sessions_dev, blocks * block_dev, latent_width)
    offsets = (
        jnp.arange(blocks, dtype=jnp.int32)[:, None] * (block_dev * groups)
        + inner_rank * block_dev
        + jnp.arange(block_dev, dtype=jnp.int32)[None, :]
    ).reshape(blocks * block_dev)
    inside = offsets[None, None, :] < cache_lengths[:, :, None]
    all_queries = lax.all_gather(queries, "inner", axis=2, tiled=True)
    head_group = all_queries.shape[2] // groups
    grouped = all_queries.reshape(batches, sessions_dev, groups, head_group, latent_width)
    scores = (
        jnp.einsum("msghc,mspc->gmshp", grouped, cached, preferred_element_type=jnp.float32)
        * softmax_scale
    )
    mask = inside[None, :, :, None, :]
    masked = jnp.where(mask, scores, -1e30)
    peaks = jnp.max(masked, axis=-1)
    weights = jnp.where(mask, jnp.exp(masked - peaks[..., None]), 0.0)
    totals = jnp.sum(weights, axis=-1)
    values = cached[..., :KV].astype(jnp.float32)
    partial_value = jnp.einsum(
        "gmshp,mspv->gmshv", weights, values, precision=lax.Precision.HIGHEST
    )
    all_peaks, all_totals, all_partials = (
        lax.all_to_all(
            peaks.astype(jnp.bfloat16), "inner", split_axis=0, concat_axis=0, tiled=True
        ).astype(peaks.dtype),
        lax.all_to_all(
            totals.astype(jnp.bfloat16), "inner", split_axis=0, concat_axis=0, tiled=True
        ).astype(totals.dtype),
        lax.all_to_all(
            partial_value.astype(jnp.bfloat16), "inner", split_axis=0, concat_axis=0, tiled=True
        ).astype(partial_value.dtype),
    )
    highest = jnp.max(all_peaks, axis=0)
    factor = jnp.exp(all_peaks - highest[None])
    denominator = jnp.sum(factor * all_totals, axis=0)
    numerator = jnp.sum(factor[..., None] * all_partials, axis=0)
    context = (numerator / denominator[..., None]).astype(jnp.bfloat16)
    moe_out = jnp.concatenate(
        [
            moe_round(
                hidden_states[micro : micro + 1],
                expert_ids[micro : micro + 1],
                gate_weights[micro : micro + 1],
                w_gate,
                w_up,
                w_down,
            )
            for micro in range(hidden_states.shape[0])
        ],
        axis=0,
    )
    return (context, moe_out)


def solution(mesh):
    placed = (
        P("dp", "inner", None),
        P(None, "dp", None),
        P(None, "dp"),
        P(None, "dp", "inner", None),
        P(None, "dp", "inner"),
        P(None, "dp", None),
        P(None, "dp", None),
        P("dp", None, "inner"),
        P("dp", None, "inner"),
        P("dp", "inner", None),
    )
    return jax.shard_map(
        on_device,
        mesh=mesh,
        in_specs=placed,
        out_specs=(P(None, "dp", "inner", None), P(None, "dp", "inner")),
        check_vma=False,
    )
```

profile of v0, /device:TPU:0, one launch (start us, length us, event | category | flops | bytes accessed | tf_op | source)
XLA Modules:
  0.0 223.1 jit_solution(978091534546285464)
XLA Ops:
  11.8 24.0 %all_to_all.40 = bf16[64,2,1792]{2,1,0:T(2,128)(2,1)S(1)} all-to-all(bf16[64,2,1792]{2,1,0:T(2,128)(2,1)S(1)} %reshape.448), channel_id=1, replica_groups=mesh['dp'=64,'inner'=2] {'dp'}, dimensions={0} | all-to-all | bytes 917504 | tf_op jit(solution)/shard_map/all_to_all | solution.py:41
  35.9 2.5 %all_gather.11 = bf16[128,3584]{1,0:T(8,128)(2,1)S(1)} all-gather(bf16[128,1792]{1,0:T(8,128)(2,1)S(1)} %reshape.449), channel_id=1, replica_groups=mesh['dp'=64,'inner'=2] {'inner'}, dimensions={1}, use_global_device_ids=true | all-gather | bytes 1376256 | tf_op jit(solution)/shard_map/all_gather | solution.py:43
  38.4 2.7 %fusion.9 = f32[128,512]{1,0:T(8,128)S(1)} fusion(bf16[128,3584]{1,0:T(8,128)(2,1)S(1)} %all_gather.11, bf16[1,3584,512]{2,1,0:T(8,128)(2,1)} %param.17), kind=kOutput, calls=%fused_computation.14 | convolution fusion | flops 469762048 | bytes 4849664 | tf_op jit(solution)/shard_map/dot_general | solution.py:44
  41.1 5.3 %fusion.1 = bf16[3584,128]{0,1:T(8,128)(2,1)} fusion(bf16[1,512,3584]{2,1,0:T(8,128)(2,1)} %param.19, bf16[128,3584]{1,0:T(8,128)(2,1)S(1)} %all_gather.11, bf16[1,3584,512]{2,1,0:T(8,128)(2,1)} %param.18, f32[128,512]{1,0:T(8,128)S(1)} %fusion.9), kind=kOutput, calls=%fused_computation.4 | convolution fusion | flops 940376064 | bytes 9437184 | tf_op jit(solution)/shard_map/dot_general | solution.py:48
  47.0 17.5 %all_to_all.41 = bf16[64,2,1792]{2,1,0:T(2,128)(2,1)S(1)} all-to-all(bf16[64,2,1792]{2,1,0:T(2,128)(2,1)S(1)} %reshape.443), channel_id=1, replica_groups=mesh['dp'=64,'inner'=2] {'dp'}, dimensions={0} | all-to-all | bytes 917504 | tf_op jit(solution)/shard_map/all_to_all | solution.py:41
  64.7 2.5 %all_gather.10 = bf16[128,3584]{1,0:T(8,128)(2,1)S(1)} all-gather(bf16[128,1792]{1,0:T(8,128)(2,1)S(1)} %reshape.444), channel_id=1, replica_groups=mesh['dp'=64,'inner'=2] {'inner'}, dimensions={1}, use_global_device_ids=true | all-gather | bytes 1376256 | tf_op jit(solution)/shard_map/all_gather | solution.py:43
  67.2 2.7 %fusion.11 = f32[128,512]{1,0:T(8,128)S(1)} fusion(bf16[128,3584]{1,0:T(8,128)(2,1)S(1)} %all_gather.10, bf16[1,3584,512]{2,1,0:T(8,128)(2,1)} %param.17), kind=kOutput, calls=%fused_computation.16 | convolution fusion | flops 469762048 | bytes 4849664 | tf_op jit(solution)/shard_map/dot_general | solution.py:44
  69.9 5.3 %fusion = bf16[3584,128]{0,1:T(8,128)(2,1)} fusion(bf16[1,512,3584]{2,1,0:T(8,128)(2,1)} %param.19, bf16[128,3584]{1,0:T(8,128)(2,1)S(1)} %all_gather.10, bf16[1,3584,512]{2,1,0:T(8,128)(2,1)} %param.18, f32[128,512]{1,0:T(8,128)S(1)} %fusion.11), kind=kOutput, calls=%fused_computation.3 | convolution fusion | flops 940376064 | bytes 9437184 | tf_op jit(solution)/shard_map/dot_general | solution.py:48
  75.2 2.0 reshape.450
  77.2 4.8 %all-to-all-start.7 = ((bf16[1792,64,2]{0,2,1:T(2,128)(2,1)}), bf16[1792,64,2]{0,2,1:T(2,128)(2,1)S(1)}, u32[]{:S(2)}, u32[]{:S(2)}) async-start(bf16[1792,64,2]{0,2,1:T(2,128)(2,1)} %reshape.450), calls=%async_computation.9 | async-start | bytes 917504 | tf_op jit(solution)/shard_map/all_to_all | solution.py:56
  82.0 2.0 reshape.445
  84.0 11.1 %all-to-all-done.7 = bf16[1792,64,2]{0,2,1:T(2,128)(2,1)S(1)} async-done(((bf16[1792,64,2]{0,2,1:T(2,128)(2,1)}), bf16[1792,64,2]{0,2,1:T(2,128)(2,1)S(1)}, u32[]{:S(2)}, u32[]{:S(2)}) %all-to-all-start.7) | async-done | bytes 458784 | tf_op jit(solution)/shard_map/all_to_all | solution.py:56
  95.1 4.8 %all-to-all-start.5 = ((bf16[1792,64,2]{0,2,1:T(2,128)(2,1)}), bf16[1792,64,2]{0,2,1:T(2,128)(2,1)S(1)}, u32[]{:S(2)}, u32[]{:S(2)}) async-start(bf16[1792,64,2]{0,2,1:T(2,128)(2,1)} %reshape.445), calls=%async_computation.6 | async-start | bytes 917504 | tf_op jit(solution)/shard_map/all_to_all | solution.py:56
  99.9 8.9 %copy.39 = bf16[128,32,576]{2,1,0:T(8,128)(2,1)} copy(bf16[128,32,576]{0,2,1:T(8,128)(2,1)} %param.10) | data formatting | bytes 9437184 | tf_op args[0]
  108.7 3.0 %all-to-all-done.5 = bf16[1792,64,2]{0,2,1:T(2,128)(2,1)S(1)} async-done(((bf16[1792,64,2]{0,2,1:T(2,128)(2,1)}), bf16[1792,64,2]{0,2,1:T(2,128)(2,1)S(1)}, u32[]{:S(2)}, u32[]{:S(2)}) %all-to-all-start.5) | async-done | bytes 458784 | tf_op jit(solution)/shard_map/all_to_all | solution.py:56
  111.7 7.7 %all-to-all-start = ((bf16[128,32,576]{2,1,0:T(8,128)(2,1)}), bf16[128,32,576]{2,1,0:T(8,128)(2,1)}, u32[]{:S(2)}, u32[]{:S(2)}) async-start(bf16[128,32,576]{2,1,0:T(8,128)(2,1)} %copy.39), calls=%async_computation | async-start | bytes 10485760 | tf_op jit(solution)/shard_map/all_to_all | solution.py:81
  122.1 60.9 %all-to-all-done = bf16[128,32,576]{2,1,0:T(8,128)(2,1)} async-done(((bf16[128,32,576]{2,1,0:T(8,128)(2,1)}), bf16[128,32,576]{2,1,0:T(8,128)(2,1)}, u32[]{:S(2)}, u32[]{:S(2)}) %all-to-all-start) | async-done | bytes 4718624 | tf_op jit(solution)/shard_map/all_to_all | solution.py:81
  183.0 6.0 %gather_fusion = bf16[128,32,576]{2,1,0:T(8,128)(2,1)} fusion(bf16[128,32,576]{2,1,0:T(8,128)(2,1)} %all-to-all-done, s32[1024]{0:T(1024)S(1)} %pad_clamp_fusion), kind=kCustom, calls=%fused_computation | custom fusion | bytes 9437696 | tf_op jit(solution)/shard_map/gather | solution.py:85
  189.0 5.3 %bitcast_reduce_fusion = (f32[2,2,8,64]{3,0,2,1:T(2,128)S(1)}, f32[2,8,256,2,64]{2,4,3,1,0:T(8,128)S(1)}) fusion(pred[2,8,256]{2,1,0:T(8,128)(4,1)S(1)} %broadcast_compare_fusion, bf16[2,8,256,576,1]{3,2,4,1,0:T(8,128)(2,1)} %bitcast.116, bf16[2,8,2,64,576]{4,3,2,1,0:T(8,128)(2,1)} %bitcast.120), kind=kOutput, calls=%fused_computation.29 | convolution fusion | flops 605550592 | bytes 9187328 | tf_op jit(solution)/shard_map/msghc,mspc->gmshp/dot_general | solution.py:96
  195.3 2.3 %convert_bitcast_fusion = bf16[2,2,8,64,512]{4,3,0,2,1:T(8,128)(2,1)S(1)} fusion(bf16[2,8,256,576]{3,2,1,0:T(8,128)(2,1)S(1)} %bitcast.117, f32[2,8,256,2,64]{2,4,3,1,0:T(8,128)S(1)} %get-tuple-element.15, f32[2,2,8,64]{3,0,2,1:T(2,128)S(1)} %get-tuple-element.14, pred[2,8,256]{2,1,0:T(8,128)(4,1)S(1)} %broadcast_compare_fusion), kind=kOutput, calls=%fused_computation.33 | convolution fusion | flops 3224371200 | bytes 8413184 | tf_op jit(solution)/shard_map/gmshp,mspv->gmshv/dot_general | solution.py:105
  200.0 3.7 %all_to_all.42 = bf16[2,2,512]{2,1,0:T(2,128)(2,1)S(1)} all-to-all(bf16[2,2,512]{2,1,0:T(2,128)(2,1)S(1)} %reshape.466), channel_id=1, replica_groups=mesh['dp'=64,'inner'=2] {'inner'}, dimensions={0} | all-to-all | bytes 8192 | tf_op jit(solution)/shard_map/all_to_all | solution.py:109
  203.7 3.2 %all-to-all-start.3 = ((bf16[2,2,512]{2,1,0:T(2,128)(2,1)}), bf16[2,2,512]{2,1,0:T(2,128)(2,1)S(1)}, u32[]{:S(2)}, u32[]{:S(2)}) async-start(bf16[2,2,512]{2,1,0:T(2,128)(2,1)} %reshape.468), calls=%async_computation.3 | async-start | bytes 8192 | tf_op jit(solution)/shard_map/all_to_all | solution.py:112
  208.3 3.8 %all-to-all-start.2 = ((bf16[2,2,8,64,512]{4,3,2,1,0:T(8,128)(2,1)}), bf16[2,2,8,64,512]{4,3,2,1,0:T(8,128)(2,1)S(1)}, u32[]{:S(2)}, u32[]{:S(2)}) async-start(bf16[2,2,8,64,512]{4,3,2,1,0:T(8,128)(2,1)} %copy.42), calls=%async_computation.2 | async-start | bytes 4194304 | tf_op jit(solution)/shard_map/all_to_all | solution.py:115
  212.2 2.8 %all-to-all-done.2 = bf16[2,2,8,64,512]{4,3,2,1,0:T(8,128)(2,1)S(1)} async-done(((bf16[2,2,8,64,512]{4,3,2,1,0:T(8,128)(2,1)}), bf16[2,2,8,64,512]{4,3,2,1,0:T(8,128)(2,1)S(1)}, u32[]{:S(2)}, u32[]{:S(2)}) %all-to-all-start.2) | async-done | bytes 2097184 | tf_op jit(solution)/shard_map/all_to_all | solution.py:115
  (64 shorter events, 14.6 us)
Async XLA Ops:
  7.2 68.1 %reduce-scatter.5.cloned.1.call-start = ((), (), s32[]{:S(2)}) async-start(), calls=%async_computation.12 | async-start | bytes 1376256 | tf_op jit(solution)/shard_map/reduce_scatter | solution.py:47
  41.1 5.4 %copy-start.1 = (bf16[2,8,1792]{2,1,0:T(8,128)(2,1)S(1)}, bf16[2,8,1792]{2,1,0:T(8,128)(2,1)}, u32[]{:S(2)}) copy-start(bf16[2,8,1792]{2,1,0:T(8,128)(2,1)} %param.14) | copy-start | bytes 172036
  46.4 35.6 %reduce-scatter.3.cloned.1.call-start = ((), (), s32[]{:S(2)}) async-start(), calls=%async_computation.11 | async-start | bytes 1376256 | tf_op jit(solution)/shard_map/reduce_scatter | solution.py:47
  77.2 17.9 %all-to-all-start.7 = ((bf16[1792,64,2]{0,2,1:T(2,128)(2,1)}), bf16[1792,64,2]{0,2,1:T(2,128)(2,1)S(1)}, u32[]{:S(2)}, u32[]{:S(2)}) async-start(bf16[1792,64,2]{0,2,1:T(2,128)(2,1)} %reshape.450), calls=%async_computation.9 | async-start | bytes 917504 | tf_op jit(solution)/shard_map/all_to_all | solution.py:56
  95.1 16.6 %all-to-all-start.5 = ((bf16[1792,64,2]{0,2,1:T(2,128)(2,1)}), bf16[1792,64,2]{0,2,1:T(2,128)(2,1)S(1)}, u32[]{:S(2)}, u32[]{:S(2)}) async-start(bf16[1792,64,2]{0,2,1:T(2,128)(2,1)} %reshape.445), calls=%async_computation.6 | async-start | bytes 917504 | tf_op jit(solution)/shard_map/all_to_all | solution.py:56
  108.7 11.5 %copy-start.2 = (s32[2,8,8]{2,1,0:T(8,128)S(1)}, s32[2,8,8]{2,1,0:T(8,128)}, u32[]{:S(2)}) copy-start(s32[2,8,8]{2,1,0:T(8,128)} %param.11) | copy-start | bytes 1540
  108.7 12.0 %copy-start.3 = (s32[2,8]{1,0:T(2,128)S(1)}, s32[2,8]{1,0:T(2,128)}, u32[]{:S(2)}) copy-start(s32[2,8]{1,0:T(2,128)} %param.12) | copy-start | bytes 196
  111.7 71.3 %all-to-all-start = ((bf16[128,32,576]{2,1,0:T(8,128)(2,1)}), bf16[128,32,576]{2,1,0:T(8,128)(2,1)}, u32[]{:S(2)}, u32[]{:S(2)}) async-start(bf16[128,32,576]{2,1,0:T(8,128)(2,1)} %copy.39), calls=%async_computation | async-start | bytes 10485760 | tf_op jit(solution)/shard_map/all_to_all | solution.py:81
  119.4 69.6 %all-gather.2.cloned.1.call-start = ((), (), s32[]{:S(2)}) async-start(), calls=%async_computation.10 | async-start | bytes 3932160 | tf_op jit(solution)/shard_map/all_gather | solution.py:92
  189.0 6.3 %copy-start = (bf16[128,32,576]{2,1,0:T(8,128)(2,1)S(1)}, bf16[128,32,576]{2,1,0:T(8,128)(2,1)}, u32[]{:S(2)}) copy-start(bf16[128,32,576]{2,1,0:T(8,128)(2,1)} %gather_fusion) | copy-start | bytes 14155780
  203.7 4.6 %all-to-all-start.3 = ((bf16[2,2,512]{2,1,0:T(2,128)(2,1)}), bf16[2,2,512]{2,1,0:T(2,128)(2,1)S(1)}, u32[]{:S(2)}, u32[]{:S(2)}) async-start(bf16[2,2,512]{2,1,0:T(2,128)(2,1)} %reshape.468), calls=%async_computation.3 | async-start | bytes 8192 | tf_op jit(solution)/shard_map/all_to_all | solution.py:112
  208.3 6.6 %all-to-all-start.2 = ((bf16[2,2,8,64,512]{4,3,2,1,0:T(8,128)(2,1)}), bf16[2,2,8,64,512]{4,3,2,1,0:T(8,128)(2,1)S(1)}, u32[]{:S(2)}, u32[]{:S(2)}) async-start(bf16[2,2,8,64,512]{4,3,2,1,0:T(8,128)(2,1)} %copy.42), calls=%async_computation.2 | async-start | bytes 4194304 | tf_op jit(solution)/shard_map/all_to_all | solution.py:115
Sparse Core Ops, SparseCore 0:
  46.6 6.6 reduce-scatter.4
  75.3 6.6 reduce-scatter.2
  121.9 15.2 all-gather.1
where the time goes:
time: 226 us; the launch traced here: 223 us
  waiting for transfers between devices  79.6 us (35%)
  blocking collectives  50.1 us (22%)
  matrix products  25.8 us (11%)
  starting transfers between devices  24.5 us (11%)
  local copies, waits for them, and re-layouts  24.1 us (11%)
  between operations  14 us (6%)
  other arithmetic  4.97 us (2%)
    all_to_all x1, waiting for transfers between devices, on_device(): lax.all_to_all(latent_pool, 'dp', split_axis=0, concat_axis=0, tiled=True)  60.9 us
    all_to_all x2, blocking collectives, moe_round(): lax.all_to_all(outgoing, 'dp', split_axis=0, concat_axis=0, tiled=True)  41.5 us
    all_to_all x2, waiting for transfers between devices, moe_round(): lax.all_to_all(outbound, 'dp', split_axis=1, concat_axis=1, tiled=True)  14.1 us
    dot_general x2, matrix products, moe_round(): lax.dot_general(down_rows, hidden, (((0,), (1,)), ((), ())), preferred_el...  10.7 us
    unnamed x13, local copies, waits for them, and re-layouts  9.81 us
    all_to_all x2, starting transfers between devices, moe_round(): lax.all_to_all(outbound, 'dp', split_axis=1, concat_axis=1, tiled=True)  9.52 us
    all_to_all x1, starting transfers between devices, on_device(): lax.all_to_all(latent_pool, 'dp', split_axis=0, concat_axis=0, tiled=True)  7.74 us
    gather x1, local copies, waits for them, and re-layouts, on_device(): resident[block_table]  5.99 us
  transfers between devices with their start and end apart: 8, of which 6 were waited for; matrix products, arithmetic and copies ran while one was open for 13% of the time, Pallas kernels for 0%

commit v1 on v0

v1 whole, which is shorter than its diff:
```python
import functools

import jax
import jax.numpy as jnp
from jax import lax
from jax.experimental import pallas as pl
from jax.experimental.pallas import tpu as pltpu
from jax.sharding import PartitionSpec as P

MESH = pl.DeviceIdType.MESH
BF16, F32 = jnp.bfloat16, jnp.float32
SCALE = 192 ** (-0.5)
N = 64
POS = 32
KV, TAIL = 512, 64
SLOT = 144
SESS = 16
HEADS = 64
ROW = 16
CHUNK = 512
SLICE = 1792
NEG = -1e30
WIDTHS = (512, 512, 512, 256)
DIST = (0, 1, 2, 1)


def dot(a, b):
    return jnp.dot(a, b, preferred_element_type=F32)


def dot_t(a, b):
    return lax.dot_general(a, b, (((1,), (1,)), ((), ())), preferred_element_type=F32)


def target_orders():
    every = [(i % 4, i // 4 % 4, i // 16) for i in range(1, N)]
    kind = lambda o: tuple(sorted((DIST[a] for a in o), reverse=True))
    flip = lambda o: tuple(-a % 4 for a in o)
    turn = lambda o: (o[1], o[2], o[0])
    order = []
    for k in sorted({kind(o) for o in every}, key=lambda k: (-sum(k), k)):
        seen = []
        for o in every:
            if kind(o) != k or o in seen:
                continue
            for _ in range(3):
                for q in (o, flip(o)):
                    if q not in seen:
                        seen.append(q)
                o = turn(o)
        order += seen
    return order, [turn(o) for o in order]


ORDERS = target_orders()


def iota(shape, dim):
    return lax.broadcasted_iota(jnp.int32, shape, dim)


def kernel(
    table, lengths, pool, queries, tokens, ids, gates, w_gate, w_up, w_down,
    context, moe,
    raw, wide, packed, resident, q_all, wg, wu, wd, out_rows, in_rows, in_other,
    share_out, share_in, back_rows, ret_rows, part_own, lse_own, part_out, lse_out, part_in, lse_in,
    raw_sem, w_sem, q_sem, pool_send, pool_recv, disp_send, disp_recv, back_send, back_recv,
    pair_send, pair_recv, part_send, part_recv, lse_send, lse_recv,
):
    me = lax.axis_index("dp")
    core = lax.axis_index("inner")
    z, y, x = me // 16, me // 4 % 4, me % 4

    def shifted(o, sign):
        return (z + sign * o[2]) % 4 * 16 + (y + sign * o[1]) % 4 * 4 + (x + sign * o[0]) % 4

    def peer(i, sign):
        a, b = shifted(ORDERS[0][i], sign), shifted(ORDERS[1][i], sign)
        return a + core * (b - a)

    sibling = {"inner": 1 - core}

    loads = []
    for k in range(4):
        for half in range(2):
            rows = pl.ds(half * 16 + k * 4, 4)
            loads.append(pltpu.make_async_copy(pool.at[rows], raw.at[rows], raw_sem.at[k * 2 + half]))
    for c in loads:
        c.start()
    q_own = pltpu.make_async_copy(queries, q_all.at[0], q_sem.at[0])
    q_own.start()
    weights = [
        pltpu.make_async_copy(a, b, w_sem.at[i]) for i, (a, b) in enumerate(((w_gate, wg), (w_up, wu), (w_down, wd)))
    ]
    for c in weights:
        c.start()

    barrier = pltpu.get_barrier_semaphore()

    def greet(i, carry):
        pl.semaphore_signal(barrier, inc=1, device_id={"dp": (me + i) % N}, device_id_type=MESH)
        return carry

    lax.fori_loop(1, N, greet, 0)
    pl.semaphore_signal(barrier, inc=1, device_id=sibling, device_id_type=MESH)

    experts = iota((SESS, N), 1)
    member, weight = jnp.zeros((SESS, N), F32), jnp.zeros((SESS, N), F32)
    for k in range(8):
        same = ids[:, k : k + 1] == experts
        member += jnp.where(same, 1.0, 0.0)
        weight += jnp.where(same, gates[:, k : k + 1], 0.0)
    r, c = iota((SESS, SESS), 0), iota((SESS, SESS), 1)
    before = dot(jnp.where((c < r) & (c // 8 == r // 8), 1.0, 0.0).astype(BF16), member.astype(BF16))
    tokens4 = jnp.concatenate(
        [tokens[:, 0:512], tokens[:, 512:1024], tokens[:, 1024:1536],
         jnp.concatenate([tokens[:, 1536:1792], jnp.zeros((SESS, 256), BF16)], axis=1)], axis=0)
    picks = [jnp.where(before == j, member, 0.0) for j in range(2)]
    name = jnp.where(iota((N * ROW, N), 0) // ROW == iota((N * ROW, N), 1), 1.0, 0.0).astype(BF16)

    def spread(m):
        return jnp.concatenate([m] * 4, axis=0).astype(BF16)

    rr, cc = iota((N * ROW, N), 0), iota((N * ROW, N), 1)
    fits = (rr % ROW // 4 == cc // SESS) & (rr % 2 == cc % SESS // 8)
    chosen = jnp.where(rr % 4 // 2 == 0, dot_t(name, spread(picks[0])), dot_t(name, spread(picks[1])))
    placing = jnp.where(fits, chosen, 0.0).astype(BF16)
    out_rows[...] = dot(placing, tokens4).astype(BF16)

    eye = jnp.where(iota((128, 128), 0) == iota((128, 128), 1), 1.0, 0.0).astype(BF16)
    for k in range(4):
        loads[2 * k].wait()
        loads[2 * k + 1].wait()

        def turn(n, carry, k=k):
            j = k * 4 + n
            for jj in (j, j + 16):
                flat = dot_t(eye, raw[jj, 0:KV, :])
                for i in range(4):
                    wide[pl.ds(i * POS + jj, 128, SLOT), :] = flat[:, i * 128 : (i + 1) * 128]
            rest = jnp.concatenate([raw[j, KV:, :], raw[j + 16, KV:, :]], axis=0)
            wide[pl.ds(4 * POS + j, 128, SLOT), :] = dot_t(eye, rest)
            return carry

        lax.fori_loop(0, 4, turn, 0)

    pl.semaphore_wait(barrier, N)

    def dispatch(i):
        d = peer(i, 1)
        return pltpu.make_async_remote_copy(
            src_ref=out_rows.at[pl.ds(pl.multiple_of(d * ROW, ROW), ROW)],
            dst_ref=in_rows.at[pl.ds(pl.multiple_of(me * ROW, ROW), ROW)],
            send_sem=disp_send.at[i], recv_sem=disp_recv.at[i], device_id={"dp": d}, device_id_type=MESH)

    for i in range(N - 1):
        dispatch(i).start()
    q_own.wait()
    q_copy = pltpu.make_async_remote_copy(
        src_ref=q_all.at[0], dst_ref=q_all.at[1], send_sem=pair_send.at[0], recv_sem=pair_recv.at[0],
        device_id=sibling, device_id_type=MESH)
    q_copy.start()

    def exchange(i):
        d = peer(i, 1)
        return pltpu.make_async_remote_copy(
            src_ref=packed.at[d], dst_ref=resident.at[pl.ds(me * 2, 2)],
            send_sem=pool_send.at[i], recv_sem=pool_recv.at[i], device_id={"dp": d}, device_id_type=MESH)

    for i in range(N - 1):
        d = peer(i, 1)
        for h in range(2):
            packed[d, h] = wide[pl.ds(pl.multiple_of((d * 2 + h) * SLOT, SLOT), SLOT), :].astype(BF16)
        exchange(i).start()
    for h in range(2):
        resident[me * 2 + h] = wide[pl.ds(pl.multiple_of((me * 2 + h) * SLOT, SLOT), SLOT), :].astype(BF16)
    own = pl.ds(pl.multiple_of(me * ROW, ROW), ROW)
    in_rows[own, :] = out_rows[own, :]

    for i in range(N - 1):
        dispatch(i).wait()
    pair = pltpu.make_async_remote_copy(
        src_ref=in_rows, dst_ref=in_other, send_sem=pair_send.at[1], recv_sem=pair_recv.at[1],
        device_id=sibling, device_id_type=MESH)
    pair.start()
    r, c = iota((256, 256), 0), iota((256, 256), 1)
    order = r // 64 * 4 + r % 64 // 4 * 16 + r % 4
    gather = jnp.where(c == order, 1.0, 0.0).astype(BF16)
    scatter = jnp.where(r == c // 64 * 4 + c % 64 // 4 * 16 + c % 4, 1.0, 0.0).astype(BF16)
    for c_ in weights:
        c_.wait()
    gate_sum, up_sum = jnp.zeros((256, 512), F32), jnp.zeros((256, 512), F32)
    for side in range(2):
        if side == 1:
            pair.wait()
        rows_ref = (in_rows, in_other)[side]
        half = core if side == 0 else 1 - core
        lined = [dot(gather, rows_ref[k * 256 : (k + 1) * 256, :]).astype(BF16) for k in range(4)]
        for q, width in enumerate(WIDTHS):
            part = jnp.concatenate([lined[k][q * 64 : (q + 1) * 64, :width] for k in range(4)], axis=0)
            rows = pl.ds(pl.multiple_of(half * SLICE + q * CHUNK, 256), width)
            gate_sum += dot(part, wg[rows, :])
            up_sum += dot(part, wu[rows, :])
    hidden = (gate_sum / (1.0 + jnp.exp(-gate_sum)) * up_sum).astype(BF16)
    for q, width in enumerate(WIDTHS):
        columns = pl.ds(pl.multiple_of((1 - core) * SLICE + q * CHUNK, 256), width)
        share_out[:, q * CHUNK : q * CHUNK + width] = dot(hidden, wd[:, columns]).astype(BF16)
    share = pltpu.make_async_remote_copy(
        src_ref=share_out, dst_ref=share_in, send_sem=pair_send.at[2], recv_sem=pair_recv.at[2],
        device_id=sibling, device_id_type=MESH)
    share.start()
    mine = []
    for q, width in enumerate(WIDTHS):
        columns = pl.ds(pl.multiple_of(core * SLICE + q * CHUNK, 256), width)
        mine.append(dot(hidden, wd[:, columns]).astype(BF16))
    share.wait()
    full = []
    for q, width in enumerate(WIDTHS):
        total = (mine[q].astype(F32) + share_in[:, q * CHUNK : q * CHUNK + width].astype(F32)).astype(BF16)
        if width < CHUNK:
            total = jnp.concatenate([total, jnp.zeros((256, CHUNK - width), BF16)], axis=1)
        full.append(total)
    for k in range(4):
        stacked = jnp.concatenate([full[q][k * 64 : (k + 1) * 64] for q in range(4)], axis=0)
        back_rows[k * 256 : (k + 1) * 256, :] = dot(scatter, stacked).astype(BF16)

    def send_back(i):
        d = peer(i, 1)
        return pltpu.make_async_remote_copy(
            src_ref=back_rows.at[pl.ds(pl.multiple_of(d * ROW, ROW), ROW)],
            dst_ref=ret_rows.at[pl.ds(pl.multiple_of(me * ROW, ROW), ROW)],
            send_sem=back_send.at[i], recv_sem=back_recv.at[i], device_id={"dp": d}, device_id_type=MESH)

    for i in range(N - 1):
        send_back(i).start()
    ret_rows[own, :] = back_rows[own, :]

    q_copy.wait()
    for i in range(N - 1):
        exchange(i).wait()

    col = iota((2 * HEADS, 256), 1)
    position = col % 128 // 16 * 64 + core * POS + col // 128 * 16 + col % 16

    def parts(t):
        a = pltpu.make_async_remote_copy(
            src_ref=part_out.at[t], dst_ref=part_in.at[t], send_sem=part_send.at[t], recv_sem=part_recv.at[t],
            device_id=sibling, device_id_type=MESH)
        b = pltpu.make_async_remote_copy(
            src_ref=lse_out.at[t], dst_ref=lse_in.at[t], send_sem=lse_send.at[t], recv_sem=lse_recv.at[t],
            device_id=sibling, device_id_type=MESH)
        return a, b

    def attend(t, carry):
        low, high, rest = [], [], []
        for b in range(8):
            block = resident[table[t, b]]
            low.append(jnp.concatenate([block[i * POS : i * POS + 16] for i in range(4)], axis=1))
            high.append(jnp.concatenate([block[i * POS + 16 : i * POS + 32] for i in range(4)], axis=1))
            rest.append(block[4 * POS :])
        keys = jnp.concatenate(low + high, axis=0)
        rest = jnp.concatenate(rest, axis=0)
        q = jnp.concatenate([q_all[0, t], q_all[1, t]], axis=0)
        q_rest, blank = q[:, KV:], jnp.zeros((2 * HEADS, TAIL), BF16)
        scores = dot_t(q[:, :KV], keys) + jnp.concatenate(
            [dot_t(jnp.concatenate([q_rest, blank], axis=1), rest),
             dot_t(jnp.concatenate([blank, q_rest], axis=1), rest)], axis=1)
        inside = position < lengths[t]
        scores = jnp.where(inside, scores * SCALE, NEG)
        peak = jnp.max(scores, axis=1, keepdims=True)
        weights_ = jnp.where(inside, jnp.exp(scores - peak), 0.0)
        total = jnp.maximum(jnp.sum(weights_, axis=1, keepdims=True), 1e-30)
        value = dot(weights_.astype(BF16), keys) / total
        lse = jnp.broadcast_to(peak + jnp.log(total), (2 * HEADS, 128))
        part_own[t] = value[:HEADS]
        lse_own[t] = lse[:HEADS]
        part_out[t] = value[HEADS:].astype(BF16)
        lse_out[t] = lse[HEADS:]
        for copy in parts(t):
            copy.start()
        return carry

    lax.fori_loop(0, SESS, attend, 0)

    def merge(t, carry):
        for copy in parts(t):
            copy.wait()
        share_ = 1.0 / (1.0 + jnp.exp(lse_in[t] - lse_own[t]))
        share_ = jnp.concatenate([share_] * 4, axis=1)
        context[t] = (part_own[t] * share_ + part_in[t].astype(F32) * (1.0 - share_)).astype(BF16)
        return carry

    lax.fori_loop(0, SESS, merge, 0)

    for i in range(N - 1):
        send_back(i).wait()
    rr, cc = iota((N, N * ROW), 0), iota((N, N * ROW), 1)
    fits = (cc % ROW // 4 == rr // SESS) & (cc % 2 == rr % SESS // 8)
    shares = [jnp.where(before == j, weight, 0.0) for j in range(2)]
    total = jnp.zeros((N, CHUNK), F32)
    for level in range(2):
        tops = [s.astype(BF16) for s in shares]
        chosen = jnp.where(cc % 4 // 2 == 0, dot_t(spread(tops[0]), name), dot_t(spread(tops[1]), name))
        total += dot(jnp.where(fits, chosen, 0.0).astype(BF16), ret_rows[...])
        shares = [s - t_.astype(F32) for s, t_ in zip(shares, tops)]
    for q, width in enumerate(WIDTHS):
        moe[:, q * CHUNK : q * CHUNK + width] = total[q * SESS : (q + 1) * SESS, :width].astype(BF16)


def on_device(pool, table, lengths, queries, hidden, ids, gates, w_gate, w_up, w_down):
    vmem = pl.BlockSpec(memory_space=pltpu.VMEM)
    smem = pl.BlockSpec(memory_space=pltpu.SMEM)
    anywhere = pl.BlockSpec(memory_space=pl.ANY)
    dma = pltpu.SemaphoreType.DMA
    context, moe = pl.pallas_call(
        kernel,
        out_shape=(
            jax.ShapeDtypeStruct((SESS, HEADS, KV), BF16),
            jax.ShapeDtypeStruct((SESS, SLICE), BF16),
        ),
        in_specs=[smem, smem, anywhere, anywhere, vmem, vmem, vmem, anywhere, anywhere, anywhere],
        out_specs=(vmem, vmem),
        scratch_shapes=[
            pltpu.VMEM((POS, KV + TAIL, 128), BF16),
            pltpu.VMEM((128 * SLOT, 128), F32),
            pltpu.VMEM((N, 2, SLOT, 128), BF16),
            pltpu.VMEM((128, SLOT, 128), BF16),
            pltpu.VMEM((2, SESS, HEADS, KV + TAIL), BF16),
            pltpu.VMEM((2 * SLICE, 512), BF16),
            pltpu.VMEM((2 * SLICE, 512), BF16),
            pltpu.VMEM((512, 2 * SLICE), BF16),
            pltpu.VMEM((N * ROW, CHUNK), BF16),
            pltpu.VMEM((N * ROW, CHUNK), BF16),
            pltpu.VMEM((N * ROW, CHUNK), BF16),
            pltpu.VMEM((256, SLICE), BF16),
            pltpu.VMEM((256, SLICE), BF16),
            pltpu.VMEM((N * ROW, CHUNK), BF16),
            pltpu.VMEM((N * ROW, CHUNK), BF16),
            pltpu.VMEM((SESS, HEADS, KV), F32),
            pltpu.VMEM((SESS, HEADS, 128), F32),
            pltpu.VMEM((SESS, HEADS, KV), BF16),
            pltpu.VMEM((SESS, HEADS, 128), F32),
            pltpu.VMEM((SESS, HEADS, KV), BF16),
            pltpu.VMEM((SESS, HEADS, 128), F32),
            dma((8,)), dma((3,)), dma((1,)),
            dma((N,)), dma((N,)), dma((N,)), dma((N,)), dma((N,)), dma((N,)),
            dma((3,)), dma((3,)),
            dma((SESS,)), dma((SESS,)), dma((SESS,)), dma((SESS,)),
        ],
        compiler_params=pltpu.CompilerParams(
            collective_id=0, has_side_effects=True, vmem_limit_bytes=60 * 2**20
        ),
    )(
        table.reshape(SESS, 8), lengths.reshape(SESS), pool.transpose(1, 2, 0),
        queries.reshape(SESS, HEADS, KV + TAIL), hidden.reshape(SESS, SLICE),
        ids.reshape(SESS, 8), gates.reshape(SESS, 8), w_gate[0], w_up[0], w_down[0],
    )
    return context.reshape(2, 8, HEADS, KV), moe.reshape(2, 8, SLICE)


def solution(mesh):
    placed = (
        P("dp", "inner", None),
        P(None, "dp", None),
        P(None, "dp"),
        P(None, "dp", "inner", None),
        P(None, "dp", "inner"),
        P(None, "dp", None),
        P(None, "dp", None),
        P("dp", None, "inner"),
        P("dp", None, "inner"),
        P("dp", "inner", None),
    )
    return jax.shard_map(
        on_device,
        mesh=mesh,
        in_specs=placed,
        out_specs=(P(None, "dp", "inner", None), P(None, "dp", "inner")),
        check_vma=False,
    )
```

time: 226 us -> 109 us (0.48)
  the two profiles are of different devices: /device:TPU:0 before, /device:TPU:4 now
where the time goes in v1:
time: 109 us
  Pallas kernels  103 us (94%)
  local copies, waits for them, and re-layouts  5 us (5%)
    pallas_call x1, Pallas kernels, on_device(): pl.pallas_call(kernel, out_shape=(jax.ShapeDtypeStruct((SESS, HEADS, KV),...  103 us
    unnamed x2, local copies, waits for them, and re-layouts  3.73 us

profile of v1, /device:TPU:4, one launch (start us, length us, event | category | flops | bytes accessed | tf_op | source)
XLA Modules:
  0.0 109.0 jit_solution(13590892438339771711)
XLA Ops:
  0.6 1.3 %reshape.29.lengths = s32[16]{0:T(128)} reshape(s32[2,8]{1,0:T(2,128)} %param.12) | data formatting | bytes 128 | tf_op jit(solution)/shard_map/reshape | solution.py:354
  1.9 103.3 %shard_map.113 = (bf16[16,64,512]{2,1,0:T(8,128)(2,1)}, bf16[16,1792]{1,0:T(8,128)(2,1)}) custom-call(s32[16,8]{1,0:T(8,128)} %bitcast.19, s32[16]{0:T(128)} %reshape.29.lengths, bf16[32,576,128]{2,1,0:T(8,128)(2,1)} %bitcast.11, bf16[16,64,576]{2,1,0:T(8,128)(2,1)} %bitcast.15, bf16[16,1792]{1,0:T(8,128)(2,1)} %bitcast.17, s32[16,8]{1,0:T(8,128)} %bitcast.20, ...), custom_call_target="tpu_custom_call" | custom-call | tf_op jit(solution)/shard_map/pallas_call | solution.py:315
  105.3 2.3 %copy.23 = bf16[2,8,64,512]{3,2,1,0:T(8,128)(2,1)} copy(bf16[2,8,64,512]{3,2,1,0:T(8,128)(2,1)} %bitcast.16) | data formatting | bytes 2097152
  107.5 1.4 %copy.24 = bf16[2,8,1792]{2,1,0:T(8,128)(2,1)} copy(bf16[2,8,1792]{2,1,0:T(8,128)(2,1)} %bitcast.18) | data formatting | bytes 114688

commit v2 on v1

--- a/solution.py
+++ b/solution.py
@@ -63,7 +63,7 @@
     table, lengths, pool, queries, tokens, ids, gates, w_gate, w_up, w_down,
     context, moe,
     raw, wide, packed, resident, q_all, wg, wu, wd, out_rows, in_rows, in_other,
-    share_out, share_in, back_rows, ret_rows, part_own, lse_own, part_out, lse_out, part_in, lse_in,
+    share_out, share_in, back_rows, ret_rows, part_own, lse_own, part_out, lse_out, part_in, lse_in, shares_of,
     raw_sem, w_sem, q_sem, pool_send, pool_recv, disp_send, disp_recv, back_send, back_recv,
     pair_send, pair_recv, part_send, part_recv, lse_send, lse_recv,
 ):
@@ -79,6 +79,15 @@
         return a + core * (b - a)
 
     sibling = {"inner": 1 - core}
+
+    barrier = pltpu.get_barrier_semaphore()
+
+    def greet(i, carry):
+        pl.semaphore_signal(barrier, inc=1, device_id={"dp": (me + i) % N}, device_id_type=MESH)
+        return carry
+
+    lax.fori_loop(1, N, greet, 0)
+    pl.semaphore_signal(barrier, inc=1, device_id=sibling, device_id_type=MESH)
 
     loads = []
     for k in range(4):
@@ -95,15 +104,6 @@
     for c in weights:
         c.start()
 
-    barrier = pltpu.get_barrier_semaphore()
-
-    def greet(i, carry):
-        pl.semaphore_signal(barrier, inc=1, device_id={"dp": (me + i) % N}, device_id_type=MESH)
-        return carry
-
-    lax.fori_loop(1, N, greet, 0)
-    pl.semaphore_signal(barrier, inc=1, device_id=sibling, device_id_type=MESH)
-
     experts = iota((SESS, N), 1)
     member, weight = jnp.zeros((SESS, N), F32), jnp.zeros((SESS, N), F32)
     for k in range(8):
@@ -127,6 +127,23 @@
     placing = jnp.where(fits, chosen, 0.0).astype(BF16)
     out_rows[...] = dot(placing, tokens4).astype(BF16)
 
+    pl.semaphore_wait(barrier, N)
+
+    def dispatch(i):
+        d = peer(i, 1)
+        return pltpu.make_async_remote_copy(
+            src_ref=out_rows.at[pl.ds(pl.multiple_of(d * ROW, ROW), ROW)],
+            dst_ref=in_rows.at[pl.ds(pl.multiple_of(me * ROW, ROW), ROW)],
+            send_sem=disp_send.at[i], recv_sem=disp_recv.at[i], device_id={"dp": d}, device_id_type=MESH)
+
+    for i in range(N - 1):
+        dispatch(i).start()
+    q_own.wait()
+    q_copy = pltpu.make_async_remote_copy(
+        src_ref=q_all.at[0], dst_ref=q_all.at[1], send_sem=pair_send.at[0], recv_sem=pair_recv.at[0],
+        device_id=sibling, device_id_type=MESH)
+    q_copy.start()
+
     eye = jnp.where(iota((128, 128), 0) == iota((128, 128), 1), 1.0, 0.0).astype(BF16)
     for k in range(4):
         loads[2 * k].wait()
@@ -144,23 +161,6 @@
 
         lax.fori_loop(0, 4, turn, 0)
 
-    pl.semaphore_wait(barrier, N)
-
-    def dispatch(i):
-        d = peer(i, 1)
-        return pltpu.make_async_remote_copy(
-            src_ref=out_rows.at[pl.ds(pl.multiple_of(d * ROW, ROW), ROW)],
-            dst_ref=in_rows.at[pl.ds(pl.multiple_of(me * ROW, ROW), ROW)],
-            send_sem=disp_send.at[i], recv_sem=disp_recv.at[i], device_id={"dp": d}, device_id_type=MESH)
-
-    for i in range(N - 1):
-        dispatch(i).start()
-    q_own.wait()
-    q_copy = pltpu.make_async_remote_copy(
-        src_ref=q_all.at[0], dst_ref=q_all.at[1], send_sem=pair_send.at[0], recv_sem=pair_recv.at[0],
-        device_id=sibling, device_id_type=MESH)
-    q_copy.start()
-
     def exchange(i):
         d = peer(i, 1)
         return pltpu.make_async_remote_copy(
@@ -176,6 +176,15 @@
         resident[me * 2 + h] = wide[pl.ds(pl.multiple_of((me * 2 + h) * SLOT, SLOT), SLOT), :].astype(BF16)
     own = pl.ds(pl.multiple_of(me * ROW, ROW), ROW)
     in_rows[own, :] = out_rows[own, :]
+
+    rr, cc = iota((N, N * ROW), 0), iota((N, N * ROW), 1)
+    fits = (cc % ROW // 4 == rr // SESS) & (cc % 2 == rr % SESS // 8)
+    shares = [jnp.where(before == j, weight, 0.0) for j in range(2)]
+    for level in range(2):
+        tops = [s.astype(BF16) for s in shares]
+        picked = jnp.where(cc % 4 // 2 == 0, dot_t(spread(tops[0]), name), dot_t(spread(tops[1]), name))
+        shares_of[level] = jnp.where(fits, picked, 0.0).astype(BF16)
+        shares = [s - t_.astype(F32) for s, t_ in zip(shares, tops)]
 
     for i in range(N - 1):
         dispatch(i).wait()
@@ -232,12 +241,14 @@
             send_sem=back_send.at[i], recv_sem=back_recv.at[i], device_id={"dp": d}, device_id_type=MESH)
 
     for i in range(N - 1):
+        exchange(i).wait_send()
+    for i in range(N - 1):
         send_back(i).start()
     ret_rows[own, :] = back_rows[own, :]
 
     q_copy.wait()
     for i in range(N - 1):
-        exchange(i).wait()
+        exchange(i).wait_recv()
 
     col = iota((2 * HEADS, 256), 1)
     position = col % 128 // 16 * 64 + core * POS + col // 128 * 16 + col % 16
@@ -265,7 +276,7 @@
         scores = dot_t(q[:, :KV], keys) + jnp.concatenate(
             [dot_t(jnp.concatenate([q_rest, blank], axis=1), rest),
              dot_t(jnp.concatenate([blank, q_rest], axis=1), rest)], axis=1)
-        inside = position < lengths[t]
+        inside = position < lengths[t // 8, t % 8]
         scores = jnp.where(inside, scores * SCALE, NEG)
         peak = jnp.max(scores, axis=1, keepdims=True)
         weights_ = jnp.where(inside, jnp.exp(scores - peak), 0.0)
@@ -280,7 +291,7 @@
             copy.start()
         return carry
 
-    lax.fori_loop(0, SESS, attend, 0)
+    lax.fori_loop(0, SESS, attend, 0, unroll=2)
 
     def merge(t, carry):
         for copy in parts(t):
@@ -290,21 +301,20 @@
         context[t] = (part_own[t] * share_ + part_in[t].astype(F32) * (1.0 - share_)).astype(BF16)
         return carry
 
-    lax.fori_loop(0, SESS, merge, 0)
+    lax.fori_loop(0, SESS, merge, 0, unroll=2)
 
     for i in range(N - 1):
         send_back(i).wait()
-    rr, cc = iota((N, N * ROW), 0), iota((N, N * ROW), 1)
-    fits = (cc % ROW // 4 == rr // SESS) & (cc % 2 == rr % SESS // 8)
-    shares = [jnp.where(before == j, weight, 0.0) for j in range(2)]
     total = jnp.zeros((N, CHUNK), F32)
     for level in range(2):
-        tops = [s.astype(BF16) for s in shares]
-        chosen = jnp.where(cc % 4 // 2 == 0, dot_t(spread(tops[0]), name), dot_t(spread(tops[1]), name))
-        total += dot(jnp.where(fits, chosen, 0.0).astype(BF16), ret_rows[...])
-        shares = [s - t_.astype(F32) for s, t_ in zip(shares, tops)]
+        total += dot(shares_of[level], ret_rows[...])
     for q, width in enumerate(WIDTHS):
         moe[:, q * CHUNK : q * CHUNK + width] = total[q * SESS : (q + 1) * SESS, :width].astype(BF16)
+
+
+def finish(context_in, moe_in, context, moe):
+    context[...] = context_in[...]
+    moe[...] = moe_in[...]
 
 
 def on_device(pool, table, lengths, queries, hidden, ids, gates, w_gate, w_up, w_down):
@@ -342,6 +352,7 @@
             pltpu.VMEM((SESS, HEADS, 128), F32),
             pltpu.VMEM((SESS, HEADS, KV), BF16),
             pltpu.VMEM((SESS, HEADS, 128), F32),
+            pltpu.VMEM((2, N, N * ROW), BF16),
             dma((8,)), dma((3,)), dma((1,)),
             dma((N,)), dma((N,)), dma((N,)), dma((N,)), dma((N,)), dma((N,)),
             dma((3,)), dma((3,)),
@@ -351,10 +362,20 @@
             collective_id=0, has_side_effects=True, vmem_limit_bytes=60 * 2**20
         ),
     )(
-        table.reshape(SESS, 8), lengths.reshape(SESS), pool.transpose(1, 2, 0),
+        table.reshape(SESS, 8), lengths, pool.transpose(1, 2, 0),
         queries.reshape(SESS, HEADS, KV + TAIL), hidden.reshape(SESS, SLICE),
         ids.reshape(SESS, 8), gates.reshape(SESS, 8), w_gate[0], w_up[0], w_down[0],
     )
+    context, moe = pl.pallas_call(
+        finish,
+        out_shape=(
+            jax.ShapeDtypeStruct((SESS, HEADS, KV), BF16),
+            jax.ShapeDtypeStruct((SESS, SLICE), BF16),
+        ),
+        grid=(4,),
+        in_specs=[pl.BlockSpec((4, HEADS, KV), lambda i: (i, 0, 0)), pl.BlockSpec((SESS, SLICE), lambda i: (0, 0))],
+        out_specs=(pl.BlockSpec((4, HEADS, KV), lambda i: (i, 0, 0)), pl.BlockSpec((SESS, SLICE), lambda i: (0, 0))),
+    )(context, moe)
     return context.reshape(2, 8, HEADS, KV), moe.reshape(2, 8, SLICE)
 
 

time: 109 us -> 103 us (0.945)
  the two profiles are of different devices: /device:TPU:4 before, /device:TPU:0 now
where the time goes in v2:
time: 103 us; the launch traced here: 102 us
  Pallas kernels  101 us (98%)
    pallas_call x1, Pallas kernels, on_device(): pl.pallas_call(kernel, out_shape=(jax.ShapeDtypeStruct((SESS, HEADS, KV),...  97.5 us
    pallas_call x1, Pallas kernels, on_device(): pl.pallas_call(finish, out_shape=(jax.ShapeDtypeStruct((SESS, HEADS, KV),...  3.38 us

profile of v2, /device:TPU:0, one launch (start us, length us, event | category | flops | bytes accessed | tf_op | source)
XLA Modules:
  0.0 101.6 jit_solution(14536095371148989457)
XLA Ops:
  0.6 97.5 %shard_map.113 = (bf16[16,64,512]{2,1,0:T(8,128)(2,1)}, bf16[16,1792]{1,0:T(8,128)(2,1)}) custom-call(s32[16,8]{1,0:T(8,128)} %bitcast.17, s32[2,8]{1,0:T(2,128)} %lengths.1, bf16[32,576,128]{2,1,0:T(8,128)(2,1)} %bitcast.11, bf16[16,64,576]{2,1,0:T(8,128)(2,1)} %bitcast.15, bf16[16,1792]{1,0:T(8,128)(2,1)} %bitcast.16, s32[16,8]{1,0:T(8,128)} %bitcast.18, ...), custom_call_target="tpu_custom_call" | custom-call | tf_op jit(solution)/shard_map/pallas_call | solution.py:325
  98.2 3.4 %shard_map.114 = (bf16[16,64,512]{2,1,0:T(8,128)(2,1)}, bf16[16,1792]{1,0:T(8,128)(2,1)}) custom-call(bf16[16,64,512]{2,1,0:T(8,128)(2,1)} %get-tuple-element.6.context_in, bf16[16,1792]{1,0:T(8,128)(2,1)} %get-tuple-element.7.moe_in), custom_call_target="tpu_custom_call" | custom-call | tf_op jit(solution)/shard_map/pallas_call | solution.py:369

commit v3 on v2

--- a/solution.py
+++ b/solution.py
@@ -55,17 +55,25 @@
 ORDERS = target_orders()
 
 
+def mixed(order):
+    return [o for pair in zip(order, order[::-1]) for o in pair][: len(order)]
+
+
+POOL_ORDERS = [mixed(order) for order in ORDERS]
+BACK_ORDERS = [order[::-1] for order in ORDERS[::-1]]
+
+
 def iota(shape, dim):
     return lax.broadcasted_iota(jnp.int32, shape, dim)
 
 
 def kernel(
-    table, lengths, pool, queries, tokens, ids, gates, w_gate, w_up, w_down,
+    table_in, lengths_in, pool, queries, tokens_in, ids_in, gates_in, w_gate, w_up, w_down,
     context, moe,
-    raw, wide, packed, resident, q_all, wg, wu, wd, out_rows, in_rows, in_other,
+    table, lengths, tokens, ids, gates, merged, raw, wide, packed, resident, q_all, wg, wu, wd, out_rows, in_rows, in_other,
     share_out, share_in, back_rows, ret_rows, part_own, lse_own, part_out, lse_out, part_in, lse_in, shares_of,
     raw_sem, w_sem, q_sem, pool_send, pool_recv, disp_send, disp_recv, back_send, back_recv,
-    pair_send, pair_recv, part_send, part_recv, lse_send, lse_recv,
+    pair_send, pair_recv, part_send, part_recv, lse_send, lse_recv, near_sem, far_sem, out_sem, small_sem,
 ):
     me = lax.axis_index("dp")
     core = lax.axis_index("inner")
@@ -74,21 +82,33 @@
     def shifted(o, sign):
         return (z + sign * o[2]) % 4 * 16 + (y + sign * o[1]) % 4 * 4 + (x + sign * o[0]) % 4
 
-    def peer(i, sign):
-        a, b = shifted(ORDERS[0][i], sign), shifted(ORDERS[1][i], sign)
+    def peer(i, orders=ORDERS):
+        a, b = shifted(orders[0][i], 1), shifted(orders[1][i], 1)
         return a + core * (b - a)
 
+
     sibling = {"inner": 1 - core}
 
     barrier = pltpu.get_barrier_semaphore()
 
-    def greet(i, carry):
-        pl.semaphore_signal(barrier, inc=1, device_id={"dp": (me + i) % N}, device_id_type=MESH)
-        return carry
-
-    lax.fori_loop(1, N, greet, 0)
+    line = []
+    for k in range(1, 4):
+        line += [shifted((k, 0, 0), 1), shifted((0, k, 0), 1), shifted((0, 0, k), 1)]
+
+    def greet(semaphore):
+        for d in line:
+            pl.semaphore_signal(semaphore, inc=1, device_id={"dp": d}, device_id_type=MESH)
+
     pl.semaphore_signal(barrier, inc=1, device_id=sibling, device_id_type=MESH)
-
+    greet(barrier)
+
+    small = [
+        pltpu.make_async_copy(a, b, small_sem.at[n])
+        for n, (a, b) in enumerate(
+            ((ids_in, ids), (tokens_in, tokens), (gates_in, gates), (table_in, table), (lengths_in, lengths)))
+    ]
+    for c in small:
+        c.start()
     loads = []
     for k in range(4):
         for half in range(2):
@@ -104,6 +124,9 @@
     for c in weights:
         c.start()
 
+    for c in small:
+        c.wait()
+
     experts = iota((SESS, N), 1)
     member, weight = jnp.zeros((SESS, N), F32), jnp.zeros((SESS, N), F32)
     for k in range(8):
@@ -127,29 +150,13 @@
     placing = jnp.where(fits, chosen, 0.0).astype(BF16)
     out_rows[...] = dot(placing, tokens4).astype(BF16)
 
-    pl.semaphore_wait(barrier, N)
-
-    def dispatch(i):
-        d = peer(i, 1)
-        return pltpu.make_async_remote_copy(
-            src_ref=out_rows.at[pl.ds(pl.multiple_of(d * ROW, ROW), ROW)],
-            dst_ref=in_rows.at[pl.ds(pl.multiple_of(me * ROW, ROW), ROW)],
-            send_sem=disp_send.at[i], recv_sem=disp_recv.at[i], device_id={"dp": d}, device_id_type=MESH)
-
-    for i in range(N - 1):
-        dispatch(i).start()
-    q_own.wait()
-    q_copy = pltpu.make_async_remote_copy(
-        src_ref=q_all.at[0], dst_ref=q_all.at[1], send_sem=pair_send.at[0], recv_sem=pair_recv.at[0],
-        device_id=sibling, device_id_type=MESH)
-    q_copy.start()
-
     eye = jnp.where(iota((128, 128), 0) == iota((128, 128), 1), 1.0, 0.0).astype(BF16)
-    for k in range(4):
+
+    def regroup(k):
         loads[2 * k].wait()
         loads[2 * k + 1].wait()
 
-        def turn(n, carry, k=k):
+        def turn(n, carry):
             j = k * 4 + n
             for jj in (j, j + 16):
                 flat = dot_t(eye, raw[jj, 0:KV, :])
@@ -161,14 +168,45 @@
 
         lax.fori_loop(0, 4, turn, 0)
 
+    def dispatch(i):
+        d = peer(i)
+        return pltpu.make_async_remote_copy(
+            src_ref=out_rows.at[pl.ds(pl.multiple_of(d * ROW, ROW), ROW)],
+            dst_ref=in_rows.at[pl.ds(pl.multiple_of(me * ROW, ROW), ROW)],
+            send_sem=disp_send.at[i], recv_sem=disp_recv.at[i], device_id={"dp": d}, device_id_type=MESH)
+
+    def send_rows(moves):
+        for i in range(N - 1):
+            if sum(a > 0 for a in ORDERS[0][i]) == moves:
+                dispatch(i).start()
+
+    pl.semaphore_wait(barrier, 10)
+    greet(near_sem)
+    send_rows(1)
+    q_own.wait()
+    q_copy = pltpu.make_async_remote_copy(
+        src_ref=q_all.at[0], dst_ref=q_all.at[1], send_sem=pair_send.at[0], recv_sem=pair_recv.at[0],
+        device_id=sibling, device_id_type=MESH)
+    q_copy.start()
+
+    regroup(0)
+    pl.semaphore_wait(near_sem, 9)
+    greet(far_sem)
+    send_rows(2)
+    regroup(1)
+    pl.semaphore_wait(far_sem, 9)
+    send_rows(3)
+    regroup(2)
+    regroup(3)
+
     def exchange(i):
-        d = peer(i, 1)
+        d = peer(i, POOL_ORDERS)
         return pltpu.make_async_remote_copy(
             src_ref=packed.at[d], dst_ref=resident.at[pl.ds(me * 2, 2)],
             send_sem=pool_send.at[i], recv_sem=pool_recv.at[i], device_id={"dp": d}, device_id_type=MESH)
 
     for i in range(N - 1):
-        d = peer(i, 1)
+        d = peer(i, POOL_ORDERS)
         for h in range(2):
             packed[d, h] = wide[pl.ds(pl.multiple_of((d * 2 + h) * SLOT, SLOT), SLOT), :].astype(BF16)
         exchange(i).start()
@@ -183,7 +221,7 @@
     for level in range(2):
         tops = [s.astype(BF16) for s in shares]
         picked = jnp.where(cc % 4 // 2 == 0, dot_t(spread(tops[0]), name), dot_t(spread(tops[1]), name))
-        shares_of[level] = jnp.where(fits, picked, 0.0).astype(BF16)
+        shares_of[level * N : (level + 1) * N, :] = jnp.where(fits, picked, 0.0).astype(BF16)
         shares = [s - t_.astype(F32) for s, t_ in zip(shares, tops)]
 
     for i in range(N - 1):
@@ -234,7 +272,7 @@
         back_rows[k * 256 : (k + 1) * 256, :] = dot(scatter, stacked).astype(BF16)
 
     def send_back(i):
-        d = peer(i, 1)
+        d = peer(i, BACK_ORDERS)
         return pltpu.make_async_remote_copy(
             src_ref=back_rows.at[pl.ds(pl.multiple_of(d * ROW, ROW), ROW)],
             dst_ref=ret_rows.at[pl.ds(pl.multiple_of(me * ROW, ROW), ROW)],
@@ -298,28 +336,38 @@
             copy.wait()
         share_ = 1.0 / (1.0 + jnp.exp(lse_in[t] - lse_own[t]))
         share_ = jnp.concatenate([share_] * 4, axis=1)
-        context[t] = (part_own[t] * share_ + part_in[t].astype(F32) * (1.0 - share_)).astype(BF16)
+        merged[t] = (part_own[t] * share_ + part_in[t].astype(F32) * (1.0 - share_)).astype(BF16)
         return carry
 
     lax.fori_loop(0, SESS, merge, 0, unroll=2)
+    result = pltpu.make_async_copy(merged, context, out_sem.at[0])
+    result.start()
 
     for i in range(N - 1):
         send_back(i).wait()
-    total = jnp.zeros((N, CHUNK), F32)
-    for level in range(2):
-        total += dot(shares_of[level], ret_rows[...])
+    both = dot(shares_of[...], ret_rows[...])
+    total = both[:N] + both[N:]
     for q, width in enumerate(WIDTHS):
         moe[:, q * CHUNK : q * CHUNK + width] = total[q * SESS : (q + 1) * SESS, :width].astype(BF16)
-
-
-def finish(context_in, moe_in, context, moe):
-    context[...] = context_in[...]
-    moe[...] = moe_in[...]
+    result.wait()
+
+
+def finish(context_in, moe_in, context, moe, held, held_moe, in_sem, out_sem):
+    steps = [(context_in.at[pl.ds(2 * k, 2)], held.at[pl.ds(2 * k, 2)], context.at[pl.ds(2 * k, 2)]) for k in range(8)]
+    steps.append((moe_in, held_moe, moe))
+    loads = [pltpu.make_async_copy(a, b, in_sem.at[k]) for k, (a, b, c) in enumerate(steps)]
+    stores = [pltpu.make_async_copy(b, c, out_sem.at[k]) for k, (a, b, c) in enumerate(steps)]
+    for c in loads:
+        c.start()
+    for load, store in zip(loads, stores):
+        load.wait()
+        store.start()
+    for c in stores:
+        c.wait()
 
 
 def on_device(pool, table, lengths, queries, hidden, ids, gates, w_gate, w_up, w_down):
     vmem = pl.BlockSpec(memory_space=pltpu.VMEM)
-    smem = pl.BlockSpec(memory_space=pltpu.SMEM)
     anywhere = pl.BlockSpec(memory_space=pl.ANY)
     dma = pltpu.SemaphoreType.DMA
     context, moe = pl.pallas_call(
@@ -328,9 +376,15 @@
             jax.ShapeDtypeStruct((SESS, HEADS, KV), BF16),
             jax.ShapeDtypeStruct((SESS, SLICE), BF16),
         ),
-        in_specs=[smem, smem, anywhere, anywhere, vmem, vmem, vmem, anywhere, anywhere, anywhere],
-        out_specs=(vmem, vmem),
+        in_specs=[anywhere] * 10,
+        out_specs=(anywhere, vmem),
         scratch_shapes=[
+            pltpu.SMEM((SESS, 8), jnp.int32),
+            pltpu.SMEM((2, 8), jnp.int32),
+            pltpu.VMEM((SESS, SLICE), BF16),
+            pltpu.VMEM((SESS, 8), jnp.int32),
+            pltpu.VMEM((SESS, 8), F32),
+            pltpu.VMEM((SESS, HEADS, KV), BF16),
             pltpu.VMEM((POS, KV + TAIL, 128), BF16),
             pltpu.VMEM((128 * SLOT, 128), F32),
             pltpu.VMEM((N, 2, SLOT, 128), BF16),
@@ -352,11 +406,12 @@
             pltpu.VMEM((SESS, HEADS, 128), F32),
             pltpu.VMEM((SESS, HEADS, KV), BF16),
             pltpu.VMEM((SESS, HEADS, 128), F32),
-            pltpu.VMEM((2, N, N * ROW), BF16),
+            pltpu.VMEM((2 * N, N * ROW), BF16),
             dma((8,)), dma((3,)), dma((1,)),
             dma((N,)), dma((N,)), dma((N,)), dma((N,)), dma((N,)), dma((N,)),
             dma((3,)), dma((3,)),
             dma((SESS,)), dma((SESS,)), dma((SESS,)), dma((SESS,)),
+            pltpu.SemaphoreType.REGULAR, pltpu.SemaphoreType.REGULAR, dma((1,)), dma((5,)),
         ],
         compiler_params=pltpu.CompilerParams(
             collective_id=0, has_side_effects=True, vmem_limit_bytes=60 * 2**20
@@ -372,9 +427,11 @@
             jax.ShapeDtypeStruct((SESS, HEADS, KV), BF16),
             jax.ShapeDtypeStruct((SESS, SLICE), BF16),
         ),
-        grid=(4,),
-        in_specs=[pl.BlockSpec((4, HEADS, KV), lambda i: (i, 0, 0)), pl.BlockSpec((SESS, SLICE), lambda i: (0, 0))],
-        out_specs=(pl.BlockSpec((4, HEADS, KV), lambda i: (i, 0, 0)), pl.BlockSpec((SESS, SLICE), lambda i: (0, 0))),
+        in_specs=[anywhere, anywhere],
+        out_specs=(anywhere, anywhere),
+        scratch_shapes=[
+            pltpu.VMEM((SESS, HEADS, KV), BF16), pltpu.VMEM((SESS, SLICE), BF16), dma((9,)), dma((9,)),
+        ],
     )(context, moe)
     return context.reshape(2, 8, HEADS, KV), moe.reshape(2, 8, SLICE)
 

time: 103 us -> 100 us (0.971); the launches traced: 102 us -> 100 us
  Pallas kernels: 101 us -> 99.5 us
    pallas_call x1, Pallas kernels: 3.38 us -> 2.12 us  [on_device(): pl.pallas_call(finish, out_shape=(jax.ShapeDtypeStruct((SESS, HEADS, KV),...]
where the time goes in v3:
time: 100 us
  Pallas kernels  99.5 us (100%)
    pallas_call x1, Pallas kernels, on_device(): pl.pallas_call(kernel, out_shape=(jax.ShapeDtypeStruct((SESS, HEADS, KV),...  97.4 us
    pallas_call x1, Pallas kernels, on_device(): pl.pallas_call(finish, out_shape=(jax.ShapeDtypeStruct((SESS, HEADS, KV),...  2.12 us

profile of v3, /device:TPU:0, one launch (start us, length us, event | category | flops | bytes accessed | tf_op | source)
XLA Modules:
  0.0 100.1 jit_solution(8433736693628900529)
XLA Ops:
  0.6 97.4 %shard_map.113 = (bf16[16,64,512]{2,1,0:T(8,128)(2,1)}, bf16[16,1792]{1,0:T(8,128)(2,1)}) custom-call(s32[16,8]{1,0:T(8,128)} %bitcast.17, s32[2,8]{1,0:T(2,128)} %lengths_in.1, bf16[32,576,128]{2,1,0:T(8,128)(2,1)} %bitcast.11, bf16[16,64,576]{2,1,0:T(8,128)(2,1)} %bitcast.15, bf16[16,1792]{1,0:T(8,128)(2,1)} %bitcast.16, s32[16,8]{1,0:T(8,128)} %bitcast.18, ...), custom_call_target="tpu_custom_call" | custom-call | tf_op jit(solution)/shard_map/pallas_call | solution.py:373
  98.0 2.1 %shard_map.114 = (bf16[16,64,512]{2,1,0:T(8,128)(2,1)}, bf16[16,1792]{1,0:T(8,128)(2,1)}) custom-call(bf16[16,64,512]{2,1,0:T(8,128)(2,1)} %get-tuple-element.6.context_in, bf16[16,1792]{1,0:T(8,128)(2,1)} %get-tuple-element.7.moe_in), custom_call_target="tpu_custom_call" | custom-call | tf_op jit(solution)/shard_map/pallas_call | solution.py:424

commit v4 on v3

--- a/solution.py
+++ b/solution.py
@@ -60,7 +60,7 @@
 
 
 POOL_ORDERS = [mixed(order) for order in ORDERS]
-BACK_ORDERS = [order[::-1] for order in ORDERS[::-1]]
+BACK_ORDERS = [ORDERS[1][::-1], [tuple(-a % 4 for a in o) for o in ORDERS[0][::-1]]]
 
 
 def iota(shape, dim):

time: 100 us -> 100 us (level)
  no operation moved by 1% of the time
where the time goes in v4:
time: 100 us
  Pallas kernels  99.5 us (100%)
    pallas_call x1, Pallas kernels, on_device(): pl.pallas_call(kernel, out_shape=(jax.ShapeDtypeStruct((SESS, HEADS, KV),...  97.4 us
    pallas_call x1, Pallas kernels, on_device(): pl.pallas_call(finish, out_shape=(jax.ShapeDtypeStruct((SESS, HEADS, KV),...  2.12 us

profile of v4, /device:TPU:0, one launch (start us, length us, event | category | flops | bytes accessed | tf_op | source)
XLA Modules:
  0.0 100.1 jit_solution(3423238006920893262)
XLA Ops:
  0.6 97.4 %shard_map.113 = (bf16[16,64,512]{2,1,0:T(8,128)(2,1)}, bf16[16,1792]{1,0:T(8,128)(2,1)}) custom-call(s32[16,8]{1,0:T(8,128)} %bitcast.17, s32[2,8]{1,0:T(2,128)} %lengths_in.1, bf16[32,576,128]{2,1,0:T(8,128)(2,1)} %bitcast.11, bf16[16,64,576]{2,1,0:T(8,128)(2,1)} %bitcast.15, bf16[16,1792]{1,0:T(8,128)(2,1)} %bitcast.16, s32[16,8]{1,0:T(8,128)} %bitcast.18, ...), custom_call_target="tpu_custom_call" | custom-call | tf_op jit(solution)/shard_map/pallas_call | solution.py:373
  98.0 2.1 %shard_map.114 = (bf16[16,64,512]{2,1,0:T(8,128)(2,1)}, bf16[16,1792]{1,0:T(8,128)(2,1)}) custom-call(bf16[16,64,512]{2,1,0:T(8,128)(2,1)} %get-tuple-element.6.context_in, bf16[16,1792]{1,0:T(8,128)(2,1)} %get-tuple-element.7.moe_in), custom_call_target="tpu_custom_call" | custom-call | tf_op jit(solution)/shard_map/pallas_call | solution.py:424
